TPU v7x, 512 devices: a whole 4x4x16 slice. The times are simulated.
512 devices in a mesh: row: 16 (over x_lo, y, core), col: 32 (over x_hi, z).
Axes of the slice: x: 4 (x_hi: 2, x_lo: 2; x = x_hi * 2 + x_lo), y: 4, z: 16, core: 2. Of those that a mesh axis runs over, the one named last changes fastest.
Arguments:
- seq_ids: int32 [1024], replicated, may hold values from 0 to 3, never falling along the last dimension, each value on 1 to 512 neighbouring positions
- query_inputs: bfloat16 [1024, 8192], P('col', 'row'), may hold values from -6 to 6
- query_grads: bfloat16 [1024, 8192], P('row', 'col'), may hold values from -0.25 to 0.25
- query_act_basis: bfloat16 [8192, 8192], P('row', 'col'), may hold values from -0.0625 to 0.0625
- query_grad_basis: bfloat16 [8192, 8192], P('col', 'row'), may hold values from -0.0625 to 0.0625
- output_inputs: bfloat16 [1024, 8192], P('col', 'row'), may hold values from -6 to 6
- output_grads: bfloat16 [1024, 8192], P('row', 'col'), may hold values from -0.25 to 0.25
- output_act_basis: bfloat16 [8192, 8192], P('row', 'col'), may hold values from -0.0625 to 0.0625
- output_grad_basis: bfloat16 [8192, 8192], P('col', 'row'), may hold values from -0.0625 to 0.0625
Outputs:
- query_corr: float32 [8192, 8192], P('row', 'col')
- output_corr: float32 [8192, 8192], P('row', 'col')
Inputs may be any that keep to these rules, and one draw needn't show every extreme that they name: seq_ids never falls along the tokens; each of the 4 sequences holds 1 to 512 tokens, and one holds exactly 512.
All inputs are finite; a program needn't handle non-finite values.
Results may differ from a plain program's by a relative error of at most 0.0003.
Values may be sent and summed in bfloat16 or wider, within the bound.
No kernel may reach another device: no remote copies, remote signals or barrier semaphores. Data moves between devices by JAX's collectives and lax.ppermute only.
A program may use at most 64 MiB of HBM per device.

v0:
```python
import jax
import jax.numpy as jnp
from jax import lax
from jax.sharding import Mesh, PartitionSpec as P

SEQS = 4
ROW = ("xl", "y", "c")
Z = ("zh", "zl")
PLANE = ("xh", "xl", "y", "c")
NZ = 16
NEAR = (0, 1, -1, 2)
FAR = (0, 4, -4, 8)
TOP = 32000.0


def shift(x, by):
    if by == 0:
        return x
    return lax.ppermute(x, Z, [(i, (i + by) % NZ) for i in range(NZ)])


def swap_half(x):
    return lax.ppermute(x, "xh", [(0, 1), (1, 0)])


def pack(x):
    b, p, t, n = x.shape
    most = jnp.max(jnp.abs(x), axis=(2, 3), keepdims=True)
    step = jnp.ceil(jnp.log2(jnp.maximum(most, 1e-30)) * 64.0)
    codes = jnp.round(x * (TOP * jnp.exp2(step * (-1.0 / 64.0)))).astype(jnp.int16)
    head = jnp.broadcast_to(step.astype(jnp.int16), (b, p, 4, n))
    return jnp.concatenate([codes.reshape(b, p * t, n), head.reshape(b, 8, n)], axis=1)


def unpack(w):
    b, rows, n = w.shape
    t = (rows - 8) // 2
    step = jnp.stack([w[:, rows - 8, :1], w[:, rows - 4, :1]], axis=1).astype(jnp.float32)
    scale = jnp.exp2(step * (1.0 / 64.0)) * (1.0 / TOP)
    return w[:, : 2 * t].reshape(b, 2, t, n).astype(jnp.float32) * scale[..., None]


def roll_blocks(x, by):
    return lax.dynamic_slice_in_dim(jnp.concatenate([x, x], 0), by, x.shape[0], 0)


def reduce_scatter_z(part):

    def group(near):
        return jnp.stack([part[(near + far) % NZ] for far in FAR])

    total = group(0)
    for near in NEAR[1:]:
        total = total + unpack(shift(pack(group(near)), near))
    result = total[0]
    for index, far in enumerate(FAR[1:]):
        result = result + unpack(shift(pack(total[index + 1 : index + 2]), far))[0]
    return result


def gather_z(w):
    level = jnp.concatenate([shift(w, far) for far in FAR], 0)
    both = jnp.concatenate([shift(level, near) for near in NEAR], 0)
    offsets = [(near + far) % NZ for near in NEAR for far in FAR]
    order = [offsets.index(i) for i in range(NZ)]
    return jnp.concatenate([both[k : k + 1] for k in order], 0)


def correct(act_rot, grad_rot, seq_ids):
    running = jnp.zeros((grad_rot.shape[1], act_rot.shape[1]), jnp.float32)
    for seq in range(SEQS):
        grad_rows = jnp.where((seq_ids == seq)[:, None], grad_rot, 0.0)
        product = lax.dot_general(
            grad_rows, act_rot, (((0,), (0,)), ((), ())), precision=lax.Precision.HIGH
        )
        running = running + product * product
    return running / SEQS


def dot(a, b):
    return jnp.dot(a, b, preferred_element_type=jnp.float32)


def per_device(seq_ids, qx, qg, qa, qb, ox, og, oa, ob):
    z = lax.axis_index(Z)
    xh = lax.axis_index("xh")
    mine_first = xh == 0
    grads = jnp.stack([qg, og])
    sent = jnp.transpose(grads.reshape(2, 2, 32, 256), (1, 0, 2, 3))
    sent = jnp.broadcast_to(sent[:, None], (2, 16, 2, 32, 256)).reshape(32, 2, 32, 256)
    got = lax.all_to_all(sent, PLANE, split_axis=0, concat_axis=0, tiled=True)
    grad_basis = jnp.stack([qb, ob])
    grad_other = swap_half(grad_basis)
    inputs = lax.all_gather(jnp.stack([qx, ox])[None], Z, axis=0, tiled=True)
    act_basis = jnp.stack([qa, oa])
    act_other = swap_half(act_basis)
    got = got.reshape(2, 16, 2, 32, 256)
    g0 = roll_blocks(got[0], z)
    g1 = roll_blocks(got[1], z)
    b0 = jnp.where(mine_first, grad_basis, grad_other)
    b1 = jnp.where(mine_first, grad_other, grad_basis)
    parts = []
    for p in range(2):
        part = dot(g0[:, p].reshape(512, 256), b0[p]) + dot(g1[:, p].reshape(512, 256), b1[p])
        parts.append(part.reshape(16, 32, 512))
    part = jnp.stack(parts, 1)
    grad_mine = reduce_scatter_z(part)
    words = gather_z(pack(grad_mine[None]))
    others = swap_half(words)
    a0 = jnp.where(mine_first, act_basis, act_other)
    a1 = jnp.where(mine_first, act_other, act_basis)
    parts = []
    for p in range(2):
        rows = inputs[:, p].reshape(512, 512)
        part = jnp.concatenate([dot(rows, a0[p]), dot(rows, a1[p])], 1)
        parts.append(part.reshape(16, 32, 512))
    act_words = pack(jnp.stack(parts, 1))
    act_words = lax.all_to_all(act_words, ROW, split_axis=0, concat_axis=0, tiled=True)
    act_mine = jnp.sum(unpack(act_words), axis=0)
    act_sent = pack(jnp.stack([act_mine[:, :, :256], act_mine[:, :, 256:]]))
    act_sent = jnp.broadcast_to(act_sent[:, None], (2, 16, 72, 256)).reshape(32, 72, 256)
    act_words = lax.all_to_all(act_sent, PLANE, split_axis=0, concat_axis=0, tiled=True)
    act = jnp.transpose(unpack(act_words), (1, 0, 2, 3)).reshape(2, 1024, 256)
    low = jnp.where(mine_first, words, others)
    high = jnp.where(mine_first, others, words)
    both = jnp.stack([low, high])
    both = lax.rev(both, (1,))
    both = lax.dynamic_slice_in_dim(jnp.concatenate([both, both], 1), NZ - 1 - z, NZ, 1)
    grad = unpack(both.reshape(32, 72, 512)).reshape(2, 16, 2, 32, 512)
    grad = jnp.transpose(grad, (2, 1, 0, 3, 4)).reshape(2, 1024, 512)
    return (correct(act[0], grad[0], seq_ids), correct(act[1], grad[1], seq_ids))


def solution(mesh):
    fine = Mesh(mesh.devices.reshape(2, 4, 2, 2, 4, 4), ("xl", "y", "c", "xh", "zh", "zl"))
    row, col = (ROW, ("xh",) + Z)
    in_specs = (P(), P(col, row), P(row, col), P(row, col), P(col, row)) + (
        P(col, row),
        P(row, col),
        P(row, col),
        P(col, row),
    )
    out_specs = (P(row, col), P(row, col))
    return jax.shard_map(
        per_device, mesh=fine, in_specs=in_specs, out_specs=out_specs, check_vma=False
    )
```

profile of v0, /device:TPU:1, one launch (start us, length us, event | category | flops | bytes accessed | tf_op | source)
XLA Modules:
  0.0 297.2 jit_solution(14725430089309707744)
XLA Ops:
  9.2 10.5 %all-to-all-start = ((bf16[32,2,32,256]{3,2,1,0:T(8,128)(2,1)}), bf16[32,2,32,256]{3,2,1,0:T(8,128)(2,1)S(1)}, u32[]{:S(2)}, u32[]{:S(2)}) async-start(bf16[32,2,32,256]{3,2,1,0:T(8,128)(2,1)} %bitcast.3), calls=%async_computation | async-start | bytes 2097152 | tf_op jit(solution)/shard_map/all_to_all | solution.py:91
  19.8 4.9 %collective-permute-start = (bf16[2,256,512]{2,1,0:T(8,128)(2,1)S(1)}, bf16[2,256,512]{2,1,0:T(8,128)(2,1)}, u32[]{:S(2)}, u32[]{:S(2)}) collective-permute-start(bf16[2,256,512]{2,1,0:T(8,128)(2,1)S(1)} %pad_maximum_fusion.3), channel_id=1, source_target_pairs={{0,16},{16,0},{1,17},{17,1},{2,18},{18,2},{3,19},{19,3},{4,20},{20... | collective-permute-start | bytes 1572872 | tf_op jit(solution)/shard_map/ppermute | solution.py:23
  25.5 1.9 collective-permute-start.14
  27.5 18.6 %collective-permute-done = bf16[2,256,512]{2,1,0:T(8,128)(2,1)} collective-permute-done((bf16[2,256,512]{2,1,0:T(8,128)(2,1)S(1)}, bf16[2,256,512]{2,1,0:T(8,128)(2,1)}, u32[]{:S(2)}, u32[]{:S(2)}) %collective-permute-start) | collective-permute-done | bytes 524320 | tf_op jit(solution)/shard_map/ppermute | solution.py:23
  49.9 2.9 collective-permute-start.3
  53.6 8.2 %collective-permute-start.2 = (s16[4,72,512]{2,1,0:T(8,128)(2,1)S(1)}, s16[4,72,512]{2,1,0:T(8,128)(2,1)S(1)}, u32[]{:S(2)}, u32[]{:S(2)}) collective-permute-start(s16[4,72,512]{2,1,0:T(8,128)(2,1)S(1)} %pad_add_fusion.3), channel_id=1, source_target_pairs={{0,15},{1,0},{2,1},{3,2},{4,3},{5,4},{6,5},{7,6},{8,7},{9,8},{10,9... | collective-permute-start | bytes 884744 | tf_op jit(solution)/shard_map/ppermute | solution.py:19
  62.5 1.9 collective-permute-start.1
  64.4 2.7 collective-permute-done.3
  67.8 11.0 %collective-permute-done.1 = s16[4,72,512]{2,1,0:T(8,128)(2,1)} collective-permute-done((s16[4,72,512]{2,1,0:T(8,128)(2,1)S(1)}, s16[4,72,512]{2,1,0:T(8,128)(2,1)}, u32[]{:S(2)}, u32[]{:S(2)}) %collective-permute-start.1) | collective-permute-done | bytes 294944 | tf_op jit(solution)/shard_map/ppermute | solution.py:19
  81.9 9.4 %collective-permute-start.6 = (s16[1,72,512]{2,1,0:T(8,128)(2,1)S(1)}, s16[1,72,512]{2,1,0:T(8,128)(2,1)S(1)}, u32[]{:S(2)}, u32[]{:S(2)}) collective-permute-start(s16[1,72,512]{2,1,0:T(8,128)(2,1)S(1)} %pad_add_fusion.8), channel_id=1, source_target_pairs={{0,8},{1,9},{2,10},{3,11},{4,12},{5,13},{6,14},{7,15},{8,0},{9,1},... | collective-permute-start | bytes 221192 | tf_op jit(solution)/shard_map/ppermute | solution.py:19
  91.6 1.9 collective-permute-start.5
  93.9 7.3 %collective-permute-start.4 = (s16[1,72,512]{2,1,0:T(8,128)(2,1)S(1)}, s16[1,72,512]{2,1,0:T(8,128)(2,1)S(1)}, u32[]{:S(2)}, u32[]{:S(2)}) collective-permute-start(s16[1,72,512]{2,1,0:T(8,128)(2,1)S(1)} %pad_add_fusion.6), channel_id=1, source_target_pairs={{0,4},{1,5},{2,6},{3,7},{4,8},{5,9},{6,10},{7,11},{8,12},{9,13},{1... | collective-permute-start | bytes 221192 | tf_op jit(solution)/shard_map/ppermute | solution.py:19
  103.1 2.1 collective-permute-done.5
  111.1 9.1 %collective-permute-start.9 = (s16[1,72,512]{2,1,0:T(8,128)(2,1)S(1)}, s16[1,72,512]{2,1,0:T(8,128)(2,1)S(1)}, u32[]{:S(2)}, u32[]{:S(2)}) collective-permute-start(s16[1,72,512]{2,1,0:T(8,128)(2,1)S(1)} %get-tuple-element.74), channel_id=1, source_target_pairs={{0,8},{1,9},{2,10},{3,11},{4,12},{5,13},{6,14},{7,15},{8,0},{9,1},... | collective-permute-start | bytes 221192 | tf_op jit(solution)/shard_map/ppermute | solution.py:19
  120.2 4.1 %collective-permute-start.8 = (s16[1,72,512]{2,1,0:T(8,128)(2,1)S(1)}, s16[1,72,512]{2,1,0:T(8,128)(2,1)S(1)}, u32[]{:S(2)}, u32[]{:S(2)}) collective-permute-start(s16[1,72,512]{2,1,0:T(8,128)(2,1)S(1)} %get-tuple-element.74), channel_id=1, source_target_pairs={{0,12},{1,13},{2,14},{3,15},{4,0},{5,1},{6,2},{7,3},{8,4},{9,5},{1... | collective-permute-start | bytes 221192 | tf_op jit(solution)/shard_map/ppermute | solution.py:19
  124.3 5.1 %collective-permute-start.7 = (s16[1,72,512]{2,1,0:T(8,128)(2,1)S(1)}, s16[1,72,512]{2,1,0:T(8,128)(2,1)S(1)}, u32[]{:S(2)}, u32[]{:S(2)}) collective-permute-start(s16[1,72,512]{2,1,0:T(8,128)(2,1)S(1)} %get-tuple-element.74), channel_id=1, source_target_pairs={{0,4},{1,5},{2,6},{3,7},{4,8},{5,9},{6,10},{7,11},{8,12},{9,13},{1... | collective-permute-start | bytes 221192 | tf_op jit(solution)/shard_map/ppermute | solution.py:19
  129.4 4.0 %collective-permute-done.8 = s16[1,72,512]{2,1,0:T(8,128)(2,1)S(1)} collective-permute-done((s16[1,72,512]{2,1,0:T(8,128)(2,1)S(1)}, s16[1,72,512]{2,1,0:T(8,128)(2,1)S(1)}, u32[]{:S(2)}, u32[]{:S(2)}) %collective-permute-start.8) | collective-permute-done | bytes 73760 | tf_op jit(solution)/shard_map/ppermute | solution.py:19
  134.1 1.9 collective-permute-start.10
  136.7 1.9 collective-permute-start.11
  139.7 4.6 %collective-permute-start.12 = (s16[4,72,512]{2,1,0:T(8,128)(2,1)S(1)}, s16[4,72,512]{2,1,0:T(8,128)(2,1)S(1)}, u32[]{:S(2)}, u32[]{:S(2)}) collective-permute-start(s16[4,72,512]{2,1,0:T(8,128)(2,1)S(1)} %pad_add_fusion.5), channel_id=1, source_target_pairs={{0,15},{1,0},{2,1},{3,2},{4,3},{5,4},{6,5},{7,6},{8,7},{9,8},{10,9... | collective-permute-start | bytes 884744 | tf_op jit(solution)/shard_map/ppermute | solution.py:19
  145.0 10.1 %collective-permute-done.11 = s16[4,72,512]{2,1,0:T(8,128)(2,1)S(1)} collective-permute-done((s16[4,72,512]{2,1,0:T(8,128)(2,1)S(1)}, s16[4,72,512]{2,1,0:T(8,128)(2,1)S(1)}, u32[]{:S(2)}, u32[]{:S(2)}) %collective-permute-start.11) | collective-permute-done | bytes 294944 | tf_op jit(solution)/shard_map/ppermute | solution.py:19
  164.0 1.9 collective-permute-start.13
  165.9 32.9 %all-gather.3.cloned.1.call-done = bf16[32,32,512]{2,1,0:T(8,128)(2,1)} async-done(((bf16[2,32,512]{2,1,0:T(8,128)(2,1)}), bf16[32,32,512]{2,1,0:T(8,128)(2,1)}) %all-gather.3.cloned.1.call-update) | async-done | bytes 1048592 | tf_op jit(solution)/shard_map/all_gather | solution.py:94
  206.7 2.0 fusion.3
  209.9 14.3 %all-to-all-start.1 = ((s16[16,72,512]{2,1,0:T(8,128)(2,1)}), s16[16,72,512]{2,1,0:T(8,128)(2,1)S(1)}, u32[]{:S(2)}, u32[]{:S(2)}) async-start(s16[16,72,512]{2,1,0:T(8,128)(2,1)} %pad_add_fusion.1), calls=%async_computation.1 | async-start | bytes 2359296 | tf_op jit(solution)/shard_map/all_to_all | solution.py:118
  226.9 2.1 select_bitcast_fusion.1
  230.8 2.7 fusion.1
  235.9 5.6 %all-to-all-done.1 = s16[16,72,512]{2,1,0:T(8,128)(2,1)S(1)} async-done(((s16[16,72,512]{2,1,0:T(8,128)(2,1)}), s16[16,72,512]{2,1,0:T(8,128)(2,1)S(1)}, u32[]{:S(2)}, u32[]{:S(2)}) %all-to-all-start.1) | async-done | bytes 1179680 | tf_op jit(solution)/shard_map/all_to_all | solution.py:118
  247.2 5.8 %all-to-all-start.2 = ((s16[32,72,256]{2,1,0:T(8,128)(2,1)}), s16[32,72,256]{2,1,0:T(8,128)(2,1)S(1)}, u32[]{:S(2)}, u32[]{:S(2)}) async-start(s16[32,72,256]{2,1,0:T(8,128)(2,1)} %bitcast.72), calls=%async_computation.2 | async-start | bytes 2359296 | tf_op jit(solution)/shard_map/all_to_all | solution.py:122
  254.8 2.3 fusion
  282.9 2.9 fusion.8
  287.7 2.7 fusion.12
  (233 shorter events, 83.2 us)
Async XLA Ops:
  7.2 12.5 %copy-start.7 = (bf16[256,512]{1,0:T(8,128)(2,1)S(1)}, bf16[256,512]{1,0:T(8,128)(2,1)}, u32[]{:S(2)}) copy-start(bf16[256,512]{1,0:T(8,128)(2,1)} %param.17) | copy-start | bytes 786436
  7.2 12.5 %copy-start.8 = (bf16[256,512]{1,0:T(8,128)(2,1)S(1)}, bf16[256,512]{1,0:T(8,128)(2,1)}, u32[]{:S(2)}) copy-start(bf16[256,512]{1,0:T(8,128)(2,1)} %param.13) | copy-start | bytes 786436
  8.0 16.6 %copy-start.9 = (bf16[512,256]{1,0:T(8,128)(2,1)S(1)}, bf16[512,256]{1,0:T(8,128)(2,1)}, u32[]{:S(2)}) copy-start(bf16[512,256]{1,0:T(8,128)(2,1)} %param.16) | copy-start | bytes 786436
  8.0 16.6 %copy-start.10 = (bf16[512,256]{1,0:T(8,128)(2,1)S(1)}, bf16[512,256]{1,0:T(8,128)(2,1)}, u32[]{:S(2)}) copy-start(bf16[512,256]{1,0:T(8,128)(2,1)} %param.12) | copy-start | bytes 786436
  9.2 38.0 %all-to-all-start = ((bf16[32,2,32,256]{3,2,1,0:T(8,128)(2,1)}), bf16[32,2,32,256]{3,2,1,0:T(8,128)(2,1)S(1)}, u32[]{:S(2)}, u32[]{:S(2)}) async-start(bf16[32,2,32,256]{3,2,1,0:T(8,128)(2,1)} %bitcast.3), calls=%async_computation | async-start | bytes 2097152 | tf_op jit(solution)/shard_map/all_to_all | solution.py:91
  19.6 179.2 %all-gather.3.cloned.1.call-start = ((), (), s32[]{:S(2)}) async-start(), calls=%async_computation.3 | async-start | bytes 1114112 | tf_op jit(solution)/shard_map/all_gather | solution.py:94
  19.8 26.3 %collective-permute-start = (bf16[2,256,512]{2,1,0:T(8,128)(2,1)S(1)}, bf16[2,256,512]{2,1,0:T(8,128)(2,1)}, u32[]{:S(2)}, u32[]{:S(2)}) collective-permute-start(bf16[2,256,512]{2,1,0:T(8,128)(2,1)S(1)} %pad_maximum_fusion.3), channel_id=1, source_target_pairs={{0,16},{16,0},{1,17},{17,1},{2,18},{18,2},{3,19},{19,3},{4,20},{20... | collective-permute-start | bytes 1572872 | tf_op jit(solution)/shard_map/ppermute | solution.py:23
  25.5 113.1 %collective-permute-start.14 = (bf16[2,512,256]{2,1,0:T(8,128)(2,1)}, bf16[2,512,256]{2,1,0:T(8,128)(2,1)}, u32[]{:S(2)}, u32[]{:S(2)}) collective-permute-start(bf16[2,512,256]{2,1,0:T(8,128)(2,1)} %pad_maximum_fusion.4), channel_id=1, source_target_pairs={{0,16},{16,0},{1,17},{17,1},{2,18},{18,2},{3,19},{19,3},{4,20},{20... | collective-permute-start | bytes 1572872 | tf_op jit(solution)/shard_map/ppermute | solution.py:23
  49.9 17.1 %collective-permute-start.3 = (s16[4,72,512]{2,1,0:T(8,128)(2,1)S(1)}, s16[4,72,512]{2,1,0:T(8,128)(2,1)S(1)}, u32[]{:S(2)}, u32[]{:S(2)}) collective-permute-start(s16[4,72,512]{2,1,0:T(8,128)(2,1)S(1)} %pad_add_fusion.4), channel_id=1, source_target_pairs={{0,2},{1,3},{2,4},{3,5},{4,6},{5,7},{6,8},{7,9},{8,10},{9,11},{10,... | collective-permute-start | bytes 884744 | tf_op jit(solution)/shard_map/ppermute | solution.py:19
  53.6 13.8 %collective-permute-start.2 = (s16[4,72,512]{2,1,0:T(8,128)(2,1)S(1)}, s16[4,72,512]{2,1,0:T(8,128)(2,1)S(1)}, u32[]{:S(2)}, u32[]{:S(2)}) collective-permute-start(s16[4,72,512]{2,1,0:T(8,128)(2,1)S(1)} %pad_add_fusion.3), channel_id=1, source_target_pairs={{0,15},{1,0},{2,1},{3,2},{4,3},{5,4},{6,5},{7,6},{8,7},{9,8},{10,9... | collective-permute-start | bytes 884744 | tf_op jit(solution)/shard_map/ppermute | solution.py:19
  62.5 16.3 %collective-permute-start.1 = (s16[4,72,512]{2,1,0:T(8,128)(2,1)S(1)}, s16[4,72,512]{2,1,0:T(8,128)(2,1)}, u32[]{:S(2)}, u32[]{:S(2)}) collective-permute-start(s16[4,72,512]{2,1,0:T(8,128)(2,1)S(1)} %pad_add_fusion.2), channel_id=1, source_target_pairs={{0,1},{1,2},{2,3},{3,4},{4,5},{5,6},{6,7},{7,8},{8,9},{9,10},{10,1... | collective-permute-start | bytes 884744 | tf_op jit(solution)/shard_map/ppermute | solution.py:19
  81.3 54.7 %copy-start.11 = (bf16[32,512]{1,0:T(8,128)(2,1)S(1)}, bf16[32,512]{1,0:T(8,128)(2,1)}, u32[]{:S(2)}) copy-start(bf16[32,512]{1,0:T(8,128)(2,1)} %param.14) | copy-start | bytes 98308
  81.3 54.7 %copy-start.12 = (bf16[32,512]{1,0:T(8,128)(2,1)S(1)}, bf16[32,512]{1,0:T(8,128)(2,1)}, u32[]{:S(2)}) copy-start(bf16[32,512]{1,0:T(8,128)(2,1)} %param.10) | copy-start | bytes 98308
  81.9 19.2 %collective-permute-start.6 = (s16[1,72,512]{2,1,0:T(8,128)(2,1)S(1)}, s16[1,72,512]{2,1,0:T(8,128)(2,1)S(1)}, u32[]{:S(2)}, u32[]{:S(2)}) collective-permute-start(s16[1,72,512]{2,1,0:T(8,128)(2,1)S(1)} %pad_add_fusion.8), channel_id=1, source_target_pairs={{0,8},{1,9},{2,10},{3,11},{4,12},{5,13},{6,14},{7,15},{8,0},{9,1},... | collective-permute-start | bytes 221192 | tf_op jit(solution)/shard_map/ppermute | solution.py:19
  91.6 13.6 %collective-permute-start.5 = (s16[1,72,512]{2,1,0:T(8,128)(2,1)S(1)}, s16[1,72,512]{2,1,0:T(8,128)(2,1)S(1)}, u32[]{:S(2)}, u32[]{:S(2)}) collective-permute-start(s16[1,72,512]{2,1,0:T(8,128)(2,1)S(1)} %pad_add_fusion.7), channel_id=1, source_target_pairs={{0,12},{1,13},{2,14},{3,15},{4,0},{5,1},{6,2},{7,3},{8,4},{9,5},{1... | collective-permute-start | bytes 221192 | tf_op jit(solution)/shard_map/ppermute | solution.py:19
  93.9 14.0 %collective-permute-start.4 = (s16[1,72,512]{2,1,0:T(8,128)(2,1)S(1)}, s16[1,72,512]{2,1,0:T(8,128)(2,1)S(1)}, u32[]{:S(2)}, u32[]{:S(2)}) collective-permute-start(s16[1,72,512]{2,1,0:T(8,128)(2,1)S(1)} %pad_add_fusion.6), channel_id=1, source_target_pairs={{0,4},{1,5},{2,6},{3,7},{4,8},{5,9},{6,10},{7,11},{8,12},{9,13},{1... | collective-permute-start | bytes 221192 | tf_op jit(solution)/shard_map/ppermute | solution.py:19
  111.1 18.3 %collective-permute-start.9 = (s16[1,72,512]{2,1,0:T(8,128)(2,1)S(1)}, s16[1,72,512]{2,1,0:T(8,128)(2,1)S(1)}, u32[]{:S(2)}, u32[]{:S(2)}) collective-permute-start(s16[1,72,512]{2,1,0:T(8,128)(2,1)S(1)} %get-tuple-element.74), channel_id=1, source_target_pairs={{0,8},{1,9},{2,10},{3,11},{4,12},{5,13},{6,14},{7,15},{8,0},{9,1},... | collective-permute-start | bytes 221192 | tf_op jit(solution)/shard_map/ppermute | solution.py:19
  120.2 13.2 %collective-permute-start.8 = (s16[1,72,512]{2,1,0:T(8,128)(2,1)S(1)}, s16[1,72,512]{2,1,0:T(8,128)(2,1)S(1)}, u32[]{:S(2)}, u32[]{:S(2)}) collective-permute-start(s16[1,72,512]{2,1,0:T(8,128)(2,1)S(1)} %get-tuple-element.74), channel_id=1, source_target_pairs={{0,12},{1,13},{2,14},{3,15},{4,0},{5,1},{6,2},{7,3},{8,4},{9,5},{1... | collective-permute-start | bytes 221192 | tf_op jit(solution)/shard_map/ppermute | solution.py:19
  124.3 9.8 %collective-permute-start.7 = (s16[1,72,512]{2,1,0:T(8,128)(2,1)S(1)}, s16[1,72,512]{2,1,0:T(8,128)(2,1)S(1)}, u32[]{:S(2)}, u32[]{:S(2)}) collective-permute-start(s16[1,72,512]{2,1,0:T(8,128)(2,1)S(1)} %get-tuple-element.74), channel_id=1, source_target_pairs={{0,4},{1,5},{2,6},{3,7},{4,8},{5,9},{6,10},{7,11},{8,12},{9,13},{1... | collective-permute-start | bytes 221192 | tf_op jit(solution)/shard_map/ppermute | solution.py:19
  134.1 10.3 %collective-permute-start.10 = (s16[4,72,512]{2,1,0:T(8,128)(2,1)S(1)}, s16[4,72,512]{2,1,0:T(8,128)(2,1)S(1)}, u32[]{:S(2)}, u32[]{:S(2)}) collective-permute-start(s16[4,72,512]{2,1,0:T(8,128)(2,1)S(1)} %pad_add_fusion.5), channel_id=1, source_target_pairs={{0,1},{1,2},{2,3},{3,4},{4,5},{5,6},{6,7},{7,8},{8,9},{9,10},{10,1... | collective-permute-start | bytes 884744 | tf_op jit(solution)/shard_map/ppermute | solution.py:19
  136.7 18.4 %collective-permute-start.11 = (s16[4,72,512]{2,1,0:T(8,128)(2,1)S(1)}, s16[4,72,512]{2,1,0:T(8,128)(2,1)S(1)}, u32[]{:S(2)}, u32[]{:S(2)}) collective-permute-start(s16[4,72,512]{2,1,0:T(8,128)(2,1)S(1)} %pad_add_fusion.5), channel_id=1, source_target_pairs={{0,2},{1,3},{2,4},{3,5},{4,6},{5,7},{6,8},{7,9},{8,10},{9,11},{10,... | collective-permute-start | bytes 884744 | tf_op jit(solution)/shard_map/ppermute | solution.py:19
  139.7 16.0 %collective-permute-start.12 = (s16[4,72,512]{2,1,0:T(8,128)(2,1)S(1)}, s16[4,72,512]{2,1,0:T(8,128)(2,1)S(1)}, u32[]{:S(2)}, u32[]{:S(2)}) collective-permute-start(s16[4,72,512]{2,1,0:T(8,128)(2,1)S(1)} %pad_add_fusion.5), channel_id=1, source_target_pairs={{0,15},{1,0},{2,1},{3,2},{4,3},{5,4},{6,5},{7,6},{8,7},{9,8},{10,9... | collective-permute-start | bytes 884744 | tf_op jit(solution)/shard_map/ppermute | solution.py:19
  164.0 62.9 %collective-permute-start.13 = (s16[16,72,512]{2,1,0:T(8,128)(2,1)}, s16[16,72,512]{2,1,0:T(8,128)(2,1)}, u32[]{:S(2)}, u32[]{:S(2)}) collective-permute-start(s16[16,72,512]{2,1,0:T(8,128)(2,1)} %slice_dynamic-update-slice_fusion), channel_id=1, source_target_pairs={{0,16},{16,0},{1,17},{17,1},{2,18},{18,2},{3,19},{19,3},{4,20},{20... | collective-permute-start | bytes 3538952 | tf_op jit(solution)/shard_map/ppermute | solution.py:23
  208.8 15.4 %copy-start.17 = (s32[1024]{0:T(1024)S(1)}, s32[1024]{0:T(1024)}, u32[]{:S(2)}) copy-start(s32[1024]{0:T(1024)} %param.9) | copy-start | bytes 12292
  209.9 31.6 %all-to-all-start.1 = ((s16[16,72,512]{2,1,0:T(8,128)(2,1)}), s16[16,72,512]{2,1,0:T(8,128)(2,1)S(1)}, u32[]{:S(2)}, u32[]{:S(2)}) async-start(s16[16,72,512]{2,1,0:T(8,128)(2,1)} %pad_add_fusion.1), calls=%async_computation.1 | async-start | bytes 2359296 | tf_op jit(solution)/shard_map/all_to_all | solution.py:118
  245.5 7.6 %copy-start.18 = (s16[2,16,1]{1,0,2:T(2,128)(2,1)S(1)}, s16[2,16,1]{1,0,2:T(2,128)(2,1)}, u32[]{:S(2)}) copy-start(s16[2,16,1]{1,0,2:T(2,128)(2,1)} %stack.221) | copy-start | bytes 196
  245.5 7.6 %copy-start.19 = (s16[2,16,1]{1,0,2:T(2,128)(2,1)S(1)}, s16[2,16,1]{1,0,2:T(2,128)(2,1)}, u32[]{:S(2)}) copy-start(s16[2,16,1]{1,0,2:T(2,128)(2,1)} %stack.220) | copy-start | bytes 196
  247.2 24.2 %all-to-all-start.2 = ((s16[32,72,256]{2,1,0:T(8,128)(2,1)}), s16[32,72,256]{2,1,0:T(8,128)(2,1)S(1)}, u32[]{:S(2)}, u32[]{:S(2)}) async-start(s16[32,72,256]{2,1,0:T(8,128)(2,1)} %bitcast.72), calls=%async_computation.2 | async-start | bytes 2359296 | tf_op jit(solution)/shard_map/all_to_all | solution.py:122
  254.8 2.3 copy-start.14
  254.8 2.3 copy-start.15
  254.8 2.3 copy-start.16
  282.9 2.9 copy-start.6
  (7 other events, 13.7 us)
Sparse Core Ops, SparseCore 0:
  136.8 61.9 all-gather.2
where the time goes:
time: 299 us; the launch traced here: 297 us
  starting transfers between devices  97.5 us (33%)
  waiting for transfers between devices  89.7 us (30%)
  local copies, waits for them, and re-layouts  48.1 us (16%)
  other arithmetic  27.5 us (9%)
  matrix products  19.4 us (6%)
  between operations  15 us (5%)
    ppermute x12, starting transfers between devices, shift(): return lax.ppermute(x, Z, [(i, (i + by) % NZ) for i in range(NZ)])  58.2 us
    all_gather x1, waiting for transfers between devices, per_device(): inputs = lax.all_gather(jnp.stack([qx, ox])[None], Z, axis=0, tiled=True)  32.9 us
    ppermute x12, waiting for transfers between devices, shift(): return lax.ppermute(x, Z, [(i, (i + by) % NZ) for i in range(NZ)])  31.4 us
    ppermute x3, waiting for transfers between devices, swap_half(): return lax.ppermute(x, 'xh', [(0, 1), (1, 0)])  18.6 us
    dot_general x8, matrix products, correct(): lax.dot_general(grad_rows, act_rot, (((0,), (0,)), ((), ())), precision=l...  16.8 us
    all_to_all x1, starting transfers between devices, per_device(): lax.all_to_all(act_words, ROW, split_axis=0, concat_axis=0, tiled=True)  14.3 us
    select_n x8, local copies, waits for them, and re-layouts, correct(): grad_rows = jnp.where((seq_ids == seq)[:, None], grad_rot, 0.0)  11.3 us
    all_to_all x1, starting transfers between devices, per_device(): got = lax.all_to_all(sent, PLANE, split_axis=0, concat_axis=0, tiled=True)  10.5 us
  transfers between devices with their start and end apart: 19, of which 11 were waited for; matrix products, arithmetic and copies ran while one was open for 23% of the time, Pallas kernels for 0%

commit v1 on v0

--- a/solution.py
+++ b/solution.py
@@ -91,7 +91,11 @@
     got = lax.all_to_all(sent, PLANE, split_axis=0, concat_axis=0, tiled=True)
     grad_basis = jnp.stack([qb, ob])
     grad_other = swap_half(grad_basis)
-    inputs = lax.all_gather(jnp.stack([qx, ox])[None], Z, axis=0, tiled=True)
+    part_2 = jnp.stack([qx, ox])[None]
+    devices = lax.axis_size(Z)
+    shards = jnp.stack([part_2 for _ in range(devices)])
+    shards = lax.all_to_all(shards, Z, split_axis=0, concat_axis=0)
+    inputs = jnp.concatenate(shards, axis=0)
     act_basis = jnp.stack([qa, oa])
     act_other = swap_half(act_basis)
     got = got.reshape(2, 16, 2, 32, 256)

time: 299 us -> 303 us (1.013)
  between operations: 15 us -> 1.63 us
  starting transfers between devices: 97.5 us -> 106 us
  waiting for transfers between devices: 89.7 us -> 94.1 us
  local copies, waits for them, and re-layouts: 48.1 us -> 51.4 us
    ppermute x12, waiting for transfers between devices: 31.4 us -> 66.4 us  [shift(): return lax.ppermute(x, Z, [(i, (i + by) % NZ) for i in range(NZ)])]
    all_gather x1 -> x0, waiting for transfers between devices: 32.9 us -> none  [per_device(): inputs = lax.all_gather(jnp.stack([qx, ox])[None], Z, axis=0, tiled=True)]
    all_to_all x0 -> x1, starting transfers between devices: none -> 12.9 us  [per_device(): shards = lax.all_to_all(shards, Z, split_axis=0, concat_axis=0)]
    ppermute x12, starting transfers between devices: 58.2 us -> 54.8 us  [shift(): return lax.ppermute(x, Z, [(i, (i + by) % NZ) for i in range(NZ)])]
    unnamed x54 -> x56, local copies, waits for them, and re-layouts: 8.98 us -> 8.98 us
  transfers between devices with their start and end apart: 19 -> 19, of which waited for: 11 -> 9; matrix products, arithmetic and copies ran while one was open for 23% -> 24% of each run, Pallas kernels for 0% -> 0%
where the time goes in v1:
time: 303 us; the launch traced here: 299 us
  starting transfers between devices  106 us (35%)
  waiting for transfers between devices  94.1 us (31%)
  local copies, waits for them, and re-layouts  51.4 us (17%)
  other arithmetic  26.6 us (9%)
  matrix products  19.3 us (6%)
    ppermute x12, waiting for transfers between devices, shift(): return lax.ppermute(x, Z, [(i, (i + by) % NZ) for i in range(NZ)])  66.4 us
    ppermute x12, starting transfers between devices, shift(): return lax.ppermute(x, Z, [(i, (i + by) % NZ) for i in range(NZ)])  54.8 us
    ppermute x3, waiting for transfers between devices, swap_half(): return lax.ppermute(x, 'xh', [(0, 1), (1, 0)])  18.6 us
    dot_general x8, matrix products, correct(): lax.dot_general(grad_rows, act_rot, (((0,), (0,)), ((), ())), precision=l...  16.8 us
    all_to_all x1, starting transfers between devices, per_device(): shards = lax.all_to_all(shards, Z, split_axis=0, concat_axis=0)  12.9 us
    all_to_all x1, starting transfers between devices, per_device(): lax.all_to_all(act_words, ROW, split_axis=0, concat_axis=0, tiled=True)  11.4 us
    select_n x8, local copies, waits for them, and re-layouts, correct(): grad_rows = jnp.where((seq_ids == seq)[:, None], grad_rot, 0.0)  11.3 us
    all_to_all x1, starting transfers between devices, per_device(): got = lax.all_to_all(sent, PLANE, split_axis=0, concat_axis=0, tiled=True)  10.6 us
  transfers between devices with their start and end apart: 19, of which 9 were waited for; matrix products, arithmetic and copies ran while one was open for 24% of the time, Pallas kernels for 0%

profile of v1, /device:TPU:1, one launch (start us, length us, event | category | flops | bytes accessed | tf_op | source)
XLA Modules:
  0.0 299.1 jit_solution(10132512968905502537)
XLA Ops:
  2.6 10.6 %all-to-all-start = ((bf16[32,2,32,256]{3,2,1,0:T(8,128)(2,1)}), bf16[32,2,32,256]{3,2,1,0:T(8,128)(2,1)S(1)}, u32[]{:S(2)}, u32[]{:S(2)}) async-start(bf16[32,2,32,256]{3,2,1,0:T(8,128)(2,1)} %bitcast.3), calls=%async_computation | async-start | bytes 2097152 | tf_op jit(solution)/shard_map/all_to_all | solution.py:91
  13.3 4.9 %collective-permute-start = (bf16[2,256,512]{2,1,0:T(8,128)(2,1)S(1)}, bf16[2,256,512]{2,1,0:T(8,128)(2,1)}, u32[]{:S(2)}, u32[]{:S(2)}) collective-permute-start(bf16[2,256,512]{2,1,0:T(8,128)(2,1)S(1)} %pad_maximum_fusion.3), channel_id=1, source_target_pairs={{0,16},{16,0},{1,17},{17,1},{2,18},{18,2},{3,19},{19,3},{4,20},{20... | collective-permute-start | bytes 1572872 | tf_op jit(solution)/shard_map/ppermute | solution.py:23
  19.1 1.9 collective-permute-start.14
  21.0 18.6 %collective-permute-done = bf16[2,256,512]{2,1,0:T(8,128)(2,1)} collective-permute-done((bf16[2,256,512]{2,1,0:T(8,128)(2,1)S(1)}, bf16[2,256,512]{2,1,0:T(8,128)(2,1)}, u32[]{:S(2)}, u32[]{:S(2)}) %collective-permute-start) | collective-permute-done | bytes 524320 | tf_op jit(solution)/shard_map/ppermute | solution.py:23
  41.9 12.9 %all-to-all-start.1 = ((bf16[16,1,2,32,512]{4,3,2,1,0:T(8,128)(2,1)}), bf16[16,1,2,32,512]{4,3,2,1,0:T(8,128)(2,1)S(1)}, u32[]{:S(2)}, u32[]{:S(2)}) async-start(bf16[16,1,2,32,512]{4,3,2,1,0:T(8,128)(2,1)} %stack.229), calls=%async_computation.1 | async-start | bytes 2097152 | tf_op jit(solution)/shard_map/all_to_all | solution.py:97
  57.5 4.2 %collective-permute-start.3 = (s16[4,72,512]{2,1,0:T(8,128)(2,1)S(1)}, s16[4,72,512]{2,1,0:T(8,128)(2,1)}, u32[]{:S(2)}, u32[]{:S(2)}) collective-permute-start(s16[4,72,512]{2,1,0:T(8,128)(2,1)S(1)} %pad_add_fusion.4), channel_id=1, source_target_pairs={{0,2},{1,3},{2,4},{3,5},{4,6},{5,7},{6,8},{7,9},{8,10},{9,11},{10,... | collective-permute-start | bytes 884744 | tf_op jit(solution)/shard_map/ppermute | solution.py:19
  62.4 3.4 %collective-permute-start.2 = (s16[4,72,512]{2,1,0:T(8,128)(2,1)S(1)}, s16[4,72,512]{2,1,0:T(8,128)(2,1)}, u32[]{:S(2)}, u32[]{:S(2)}) collective-permute-start(s16[4,72,512]{2,1,0:T(8,128)(2,1)S(1)} %pad_add_fusion.3), channel_id=1, source_target_pairs={{0,15},{1,0},{2,1},{3,2},{4,3},{5,4},{6,5},{7,6},{8,7},{9,8},{10,9... | collective-permute-start | bytes 884744 | tf_op jit(solution)/shard_map/ppermute | solution.py:19
  66.6 1.9 collective-permute-start.1
  68.5 43.1 %collective-permute-done.3 = s16[4,72,512]{2,1,0:T(8,128)(2,1)} collective-permute-done((s16[4,72,512]{2,1,0:T(8,128)(2,1)S(1)}, s16[4,72,512]{2,1,0:T(8,128)(2,1)}, u32[]{:S(2)}, u32[]{:S(2)}) %collective-permute-start.3) | collective-permute-done | bytes 294944 | tf_op jit(solution)/shard_map/ppermute | solution.py:19
  113.9 8.0 %collective-permute-done.1 = s16[4,72,512]{2,1,0:T(8,128)(2,1)} collective-permute-done((s16[4,72,512]{2,1,0:T(8,128)(2,1)S(1)}, s16[4,72,512]{2,1,0:T(8,128)(2,1)}, u32[]{:S(2)}, u32[]{:S(2)}) %collective-permute-start.1) | collective-permute-done | bytes 294944 | tf_op jit(solution)/shard_map/ppermute | solution.py:19
  126.9 10.6 %collective-permute-start.6 = (s16[1,72,512]{2,1,0:T(8,128)(2,1)S(1)}, s16[1,72,512]{2,1,0:T(8,128)(2,1)S(1)}, u32[]{:S(2)}, u32[]{:S(2)}) collective-permute-start(s16[1,72,512]{2,1,0:T(8,128)(2,1)S(1)} %pad_add_fusion.8), channel_id=1, source_target_pairs={{0,8},{1,9},{2,10},{3,11},{4,12},{5,13},{6,14},{7,15},{8,0},{9,1},... | collective-permute-start | bytes 221192 | tf_op jit(solution)/shard_map/ppermute | solution.py:19
  137.8 1.9 collective-permute-start.5
  140.1 7.3 %collective-permute-start.4 = (s16[1,72,512]{2,1,0:T(8,128)(2,1)S(1)}, s16[1,72,512]{2,1,0:T(8,128)(2,1)S(1)}, u32[]{:S(2)}, u32[]{:S(2)}) collective-permute-start(s16[1,72,512]{2,1,0:T(8,128)(2,1)S(1)} %pad_add_fusion.6), channel_id=1, source_target_pairs={{0,4},{1,5},{2,6},{3,7},{4,8},{5,9},{6,10},{7,11},{8,12},{9,13},{1... | collective-permute-start | bytes 221192 | tf_op jit(solution)/shard_map/ppermute | solution.py:19
  156.8 8.0 %collective-permute-start.9 = (s16[1,72,512]{2,1,0:T(8,128)(2,1)S(1)}, s16[1,72,512]{2,1,0:T(8,128)(2,1)S(1)}, u32[]{:S(2)}, u32[]{:S(2)}) collective-permute-start(s16[1,72,512]{2,1,0:T(8,128)(2,1)S(1)} %get-tuple-element.74), channel_id=1, source_target_pairs={{0,8},{1,9},{2,10},{3,11},{4,12},{5,13},{6,14},{7,15},{8,0},{9,1},... | collective-permute-start | bytes 221192 | tf_op jit(solution)/shard_map/ppermute | solution.py:19
  164.7 5.9 %collective-permute-start.8 = (s16[1,72,512]{2,1,0:T(8,128)(2,1)S(1)}, s16[1,72,512]{2,1,0:T(8,128)(2,1)S(1)}, u32[]{:S(2)}, u32[]{:S(2)}) collective-permute-start(s16[1,72,512]{2,1,0:T(8,128)(2,1)S(1)} %get-tuple-element.74), channel_id=1, source_target_pairs={{0,12},{1,13},{2,14},{3,15},{4,0},{5,1},{6,2},{7,3},{8,4},{9,5},{1... | collective-permute-start | bytes 221192 | tf_op jit(solution)/shard_map/ppermute | solution.py:19
  170.6 3.3 %collective-permute-start.7 = (s16[1,72,512]{2,1,0:T(8,128)(2,1)S(1)}, s16[1,72,512]{2,1,0:T(8,128)(2,1)S(1)}, u32[]{:S(2)}, u32[]{:S(2)}) collective-permute-start(s16[1,72,512]{2,1,0:T(8,128)(2,1)S(1)} %get-tuple-element.74), channel_id=1, source_target_pairs={{0,4},{1,5},{2,6},{3,7},{4,8},{5,9},{6,10},{7,11},{8,12},{9,13},{1... | collective-permute-start | bytes 221192 | tf_op jit(solution)/shard_map/ppermute | solution.py:19
  173.9 6.2 %collective-permute-done.8 = s16[1,72,512]{2,1,0:T(8,128)(2,1)S(1)} collective-permute-done((s16[1,72,512]{2,1,0:T(8,128)(2,1)S(1)}, s16[1,72,512]{2,1,0:T(8,128)(2,1)S(1)}, u32[]{:S(2)}, u32[]{:S(2)}) %collective-permute-start.8) | collective-permute-done | bytes 73760 | tf_op jit(solution)/shard_map/ppermute | solution.py:19
  180.2 1.9 collective-permute-start.10
  182.1 1.9 collective-permute-start.11
  185.2 4.6 %collective-permute-start.12 = (s16[4,72,512]{2,1,0:T(8,128)(2,1)S(1)}, s16[4,72,512]{2,1,0:T(8,128)(2,1)S(1)}, u32[]{:S(2)}, u32[]{:S(2)}) collective-permute-start(s16[4,72,512]{2,1,0:T(8,128)(2,1)S(1)} %pad_add_fusion.5), channel_id=1, source_target_pairs={{0,15},{1,0},{2,1},{3,2},{4,3},{5,4},{6,5},{7,6},{8,7},{9,8},{10,9... | collective-permute-start | bytes 884744 | tf_op jit(solution)/shard_map/ppermute | solution.py:19
  190.4 6.7 %collective-permute-done.11 = s16[4,72,512]{2,1,0:T(8,128)(2,1)S(1)} collective-permute-done((s16[4,72,512]{2,1,0:T(8,128)(2,1)S(1)}, s16[4,72,512]{2,1,0:T(8,128)(2,1)S(1)}, u32[]{:S(2)}, u32[]{:S(2)}) %collective-permute-start.11) | collective-permute-done | bytes 294944 | tf_op jit(solution)/shard_map/ppermute | solution.py:19
  206.0 1.9 collective-permute-start.13
  214.7 2.0 fusion.3
  217.9 11.4 %all-to-all-start.2 = ((s16[16,72,512]{2,1,0:T(8,128)(2,1)}), s16[16,72,512]{2,1,0:T(8,128)(2,1)S(1)}, u32[]{:S(2)}, u32[]{:S(2)}) async-start(s16[16,72,512]{2,1,0:T(8,128)(2,1)} %pad_add_fusion.1), calls=%async_computation.2 | async-start | bytes 2359296 | tf_op jit(solution)/shard_map/all_to_all | solution.py:122
  232.0 2.1 select_bitcast_fusion.1
  235.9 2.7 fusion.1
  241.0 7.5 %all-to-all-done.2 = s16[16,72,512]{2,1,0:T(8,128)(2,1)S(1)} async-done(((s16[16,72,512]{2,1,0:T(8,128)(2,1)}), s16[16,72,512]{2,1,0:T(8,128)(2,1)S(1)}, u32[]{:S(2)}, u32[]{:S(2)}) %all-to-all-start.2) | async-done | bytes 1179680 | tf_op jit(solution)/shard_map/all_to_all | solution.py:122
  254.3 7.5 %all-to-all-start.3 = ((s16[32,72,256]{2,1,0:T(8,128)(2,1)}), s16[32,72,256]{2,1,0:T(8,128)(2,1)S(1)}, u32[]{:S(2)}, u32[]{:S(2)}) async-start(s16[32,72,256]{2,1,0:T(8,128)(2,1)} %bitcast.72), calls=%async_computation.3 | async-start | bytes 2359296 | tf_op jit(solution)/shard_map/all_to_all | solution.py:126
  263.6 2.3 fusion
  282.2 1.9 convolution_multiply_fusion.5
  291.7 2.9 fusion.8
  296.4 2.7 fusion.12
  (235 shorter events, 84.9 us)
Async XLA Ops:
  0.6 12.6 %copy-start.7 = (bf16[256,512]{1,0:T(8,128)(2,1)S(1)}, bf16[256,512]{1,0:T(8,128)(2,1)}, u32[]{:S(2)}) copy-start(bf16[256,512]{1,0:T(8,128)(2,1)} %param.17) | copy-start | bytes 786436
  0.6 12.6 %copy-start.8 = (bf16[256,512]{1,0:T(8,128)(2,1)S(1)}, bf16[256,512]{1,0:T(8,128)(2,1)}, u32[]{:S(2)}) copy-start(bf16[256,512]{1,0:T(8,128)(2,1)} %param.13) | copy-start | bytes 786436
  1.5 16.7 %copy-start.9 = (bf16[512,256]{1,0:T(8,128)(2,1)S(1)}, bf16[512,256]{1,0:T(8,128)(2,1)}, u32[]{:S(2)}) copy-start(bf16[512,256]{1,0:T(8,128)(2,1)} %param.16) | copy-start | bytes 786436
  1.5 16.7 %copy-start.10 = (bf16[512,256]{1,0:T(8,128)(2,1)S(1)}, bf16[512,256]{1,0:T(8,128)(2,1)}, u32[]{:S(2)}) copy-start(bf16[512,256]{1,0:T(8,128)(2,1)} %param.12) | copy-start | bytes 786436
  2.6 18.4 %copy-start.12 = (bf16[32,512]{1,0:T(8,128)(2,1)S(1)}, bf16[32,512]{1,0:T(8,128)(2,1)}, u32[]{:S(2)}) copy-start(bf16[32,512]{1,0:T(8,128)(2,1)} %param.14) | copy-start | bytes 98308
  2.6 18.4 %copy-start.13 = (bf16[32,512]{1,0:T(8,128)(2,1)S(1)}, bf16[32,512]{1,0:T(8,128)(2,1)}, u32[]{:S(2)}) copy-start(bf16[32,512]{1,0:T(8,128)(2,1)} %param.10) | copy-start | bytes 98308
  2.6 38.2 %all-to-all-start = ((bf16[32,2,32,256]{3,2,1,0:T(8,128)(2,1)}), bf16[32,2,32,256]{3,2,1,0:T(8,128)(2,1)S(1)}, u32[]{:S(2)}, u32[]{:S(2)}) async-start(bf16[32,2,32,256]{3,2,1,0:T(8,128)(2,1)} %bitcast.3), calls=%async_computation | async-start | bytes 2097152 | tf_op jit(solution)/shard_map/all_to_all | solution.py:91
  13.3 26.4 %collective-permute-start = (bf16[2,256,512]{2,1,0:T(8,128)(2,1)S(1)}, bf16[2,256,512]{2,1,0:T(8,128)(2,1)}, u32[]{:S(2)}, u32[]{:S(2)}) collective-permute-start(bf16[2,256,512]{2,1,0:T(8,128)(2,1)S(1)} %pad_maximum_fusion.3), channel_id=1, source_target_pairs={{0,16},{16,0},{1,17},{17,1},{2,18},{18,2},{3,19},{19,3},{4,20},{20... | collective-permute-start | bytes 1572872 | tf_op jit(solution)/shard_map/ppermute | solution.py:23
  19.1 165.0 %collective-permute-start.14 = (bf16[2,512,256]{2,1,0:T(8,128)(2,1)}, bf16[2,512,256]{2,1,0:T(8,128)(2,1)}, u32[]{:S(2)}, u32[]{:S(2)}) collective-permute-start(bf16[2,512,256]{2,1,0:T(8,128)(2,1)} %pad_maximum_fusion.4), channel_id=1, source_target_pairs={{0,16},{16,0},{1,17},{17,1},{2,18},{18,2},{3,19},{19,3},{4,20},{20... | collective-permute-start | bytes 1572872 | tf_op jit(solution)/shard_map/ppermute | solution.py:23
  41.9 166.1 %all-to-all-start.1 = ((bf16[16,1,2,32,512]{4,3,2,1,0:T(8,128)(2,1)}), bf16[16,1,2,32,512]{4,3,2,1,0:T(8,128)(2,1)S(1)}, u32[]{:S(2)}, u32[]{:S(2)}) async-start(bf16[16,1,2,32,512]{4,3,2,1,0:T(8,128)(2,1)} %stack.229), calls=%async_computation.1 | async-start | bytes 2097152 | tf_op jit(solution)/shard_map/all_to_all | solution.py:97
  57.5 54.1 %collective-permute-start.3 = (s16[4,72,512]{2,1,0:T(8,128)(2,1)S(1)}, s16[4,72,512]{2,1,0:T(8,128)(2,1)}, u32[]{:S(2)}, u32[]{:S(2)}) collective-permute-start(s16[4,72,512]{2,1,0:T(8,128)(2,1)S(1)} %pad_add_fusion.4), channel_id=1, source_target_pairs={{0,2},{1,3},{2,4},{3,5},{4,6},{5,7},{6,8},{7,9},{8,10},{9,11},{10,... | collective-permute-start | bytes 884744 | tf_op jit(solution)/shard_map/ppermute | solution.py:19
  62.4 50.3 %collective-permute-start.2 = (s16[4,72,512]{2,1,0:T(8,128)(2,1)S(1)}, s16[4,72,512]{2,1,0:T(8,128)(2,1)}, u32[]{:S(2)}, u32[]{:S(2)}) collective-permute-start(s16[4,72,512]{2,1,0:T(8,128)(2,1)S(1)} %pad_add_fusion.3), channel_id=1, source_target_pairs={{0,15},{1,0},{2,1},{3,2},{4,3},{5,4},{6,5},{7,6},{8,7},{9,8},{10,9... | collective-permute-start | bytes 884744 | tf_op jit(solution)/shard_map/ppermute | solution.py:19
  66.6 55.3 %collective-permute-start.1 = (s16[4,72,512]{2,1,0:T(8,128)(2,1)S(1)}, s16[4,72,512]{2,1,0:T(8,128)(2,1)}, u32[]{:S(2)}, u32[]{:S(2)}) collective-permute-start(s16[4,72,512]{2,1,0:T(8,128)(2,1)S(1)} %pad_add_fusion.2), channel_id=1, source_target_pairs={{0,1},{1,2},{2,3},{3,4},{4,5},{5,6},{6,7},{7,8},{8,9},{9,10},{10,1... | collective-permute-start | bytes 884744 | tf_op jit(solution)/shard_map/ppermute | solution.py:19
  126.3 57.8 %copy-start.11 = (bf16[512,256]{1,0:T(8,128)(2,1)S(1)}, bf16[512,256]{1,0:T(8,128)(2,1)}, u32[]{:S(2)}) copy-start(bf16[512,256]{1,0:T(8,128)(2,1)} %param.12) | copy-start | bytes 786436
  126.9 20.5 %collective-permute-start.6 = (s16[1,72,512]{2,1,0:T(8,128)(2,1)S(1)}, s16[1,72,512]{2,1,0:T(8,128)(2,1)S(1)}, u32[]{:S(2)}, u32[]{:S(2)}) collective-permute-start(s16[1,72,512]{2,1,0:T(8,128)(2,1)S(1)} %pad_add_fusion.8), channel_id=1, source_target_pairs={{0,8},{1,9},{2,10},{3,11},{4,12},{5,13},{6,14},{7,15},{8,0},{9,1},... | collective-permute-start | bytes 221192 | tf_op jit(solution)/shard_map/ppermute | solution.py:19
  137.8 13.3 %collective-permute-start.5 = (s16[1,72,512]{2,1,0:T(8,128)(2,1)S(1)}, s16[1,72,512]{2,1,0:T(8,128)(2,1)S(1)}, u32[]{:S(2)}, u32[]{:S(2)}) collective-permute-start(s16[1,72,512]{2,1,0:T(8,128)(2,1)S(1)} %pad_add_fusion.7), channel_id=1, source_target_pairs={{0,12},{1,13},{2,14},{3,15},{4,0},{5,1},{6,2},{7,3},{8,4},{9,5},{1... | collective-permute-start | bytes 221192 | tf_op jit(solution)/shard_map/ppermute | solution.py:19
  140.1 13.5 %collective-permute-start.4 = (s16[1,72,512]{2,1,0:T(8,128)(2,1)S(1)}, s16[1,72,512]{2,1,0:T(8,128)(2,1)S(1)}, u32[]{:S(2)}, u32[]{:S(2)}) collective-permute-start(s16[1,72,512]{2,1,0:T(8,128)(2,1)S(1)} %pad_add_fusion.6), channel_id=1, source_target_pairs={{0,4},{1,5},{2,6},{3,7},{4,8},{5,9},{6,10},{7,11},{8,12},{9,13},{1... | collective-permute-start | bytes 221192 | tf_op jit(solution)/shard_map/ppermute | solution.py:19
  156.8 17.2 %collective-permute-start.9 = (s16[1,72,512]{2,1,0:T(8,128)(2,1)S(1)}, s16[1,72,512]{2,1,0:T(8,128)(2,1)S(1)}, u32[]{:S(2)}, u32[]{:S(2)}) collective-permute-start(s16[1,72,512]{2,1,0:T(8,128)(2,1)S(1)} %get-tuple-element.74), channel_id=1, source_target_pairs={{0,8},{1,9},{2,10},{3,11},{4,12},{5,13},{6,14},{7,15},{8,0},{9,1},... | collective-permute-start | bytes 221192 | tf_op jit(solution)/shard_map/ppermute | solution.py:19
  164.7 15.4 %collective-permute-start.8 = (s16[1,72,512]{2,1,0:T(8,128)(2,1)S(1)}, s16[1,72,512]{2,1,0:T(8,128)(2,1)S(1)}, u32[]{:S(2)}, u32[]{:S(2)}) collective-permute-start(s16[1,72,512]{2,1,0:T(8,128)(2,1)S(1)} %get-tuple-element.74), channel_id=1, source_target_pairs={{0,12},{1,13},{2,14},{3,15},{4,0},{5,1},{6,2},{7,3},{8,4},{9,5},{1... | collective-permute-start | bytes 221192 | tf_op jit(solution)/shard_map/ppermute | solution.py:19
  170.6 9.5 %collective-permute-start.7 = (s16[1,72,512]{2,1,0:T(8,128)(2,1)S(1)}, s16[1,72,512]{2,1,0:T(8,128)(2,1)S(1)}, u32[]{:S(2)}, u32[]{:S(2)}) collective-permute-start(s16[1,72,512]{2,1,0:T(8,128)(2,1)S(1)} %get-tuple-element.74), channel_id=1, source_target_pairs={{0,4},{1,5},{2,6},{3,7},{4,8},{5,9},{6,10},{7,11},{8,12},{9,13},{1... | collective-permute-start | bytes 221192 | tf_op jit(solution)/shard_map/ppermute | solution.py:19
  180.2 9.6 %collective-permute-start.10 = (s16[4,72,512]{2,1,0:T(8,128)(2,1)S(1)}, s16[4,72,512]{2,1,0:T(8,128)(2,1)S(1)}, u32[]{:S(2)}, u32[]{:S(2)}) collective-permute-start(s16[4,72,512]{2,1,0:T(8,128)(2,1)S(1)} %pad_add_fusion.5), channel_id=1, source_target_pairs={{0,1},{1,2},{2,3},{3,4},{4,5},{5,6},{6,7},{7,8},{8,9},{9,10},{10,1... | collective-permute-start | bytes 884744 | tf_op jit(solution)/shard_map/ppermute | solution.py:19
  182.1 15.0 %collective-permute-start.11 = (s16[4,72,512]{2,1,0:T(8,128)(2,1)S(1)}, s16[4,72,512]{2,1,0:T(8,128)(2,1)S(1)}, u32[]{:S(2)}, u32[]{:S(2)}) collective-permute-start(s16[4,72,512]{2,1,0:T(8,128)(2,1)S(1)} %pad_add_fusion.5), channel_id=1, source_target_pairs={{0,2},{1,3},{2,4},{3,5},{4,6},{5,7},{6,8},{7,9},{8,10},{9,11},{10,... | collective-permute-start | bytes 884744 | tf_op jit(solution)/shard_map/ppermute | solution.py:19
  185.2 12.6 %collective-permute-start.12 = (s16[4,72,512]{2,1,0:T(8,128)(2,1)S(1)}, s16[4,72,512]{2,1,0:T(8,128)(2,1)S(1)}, u32[]{:S(2)}, u32[]{:S(2)}) collective-permute-start(s16[4,72,512]{2,1,0:T(8,128)(2,1)S(1)} %pad_add_fusion.5), channel_id=1, source_target_pairs={{0,15},{1,0},{2,1},{3,2},{4,3},{5,4},{6,5},{7,6},{8,7},{9,8},{10,9... | collective-permute-start | bytes 884744 | tf_op jit(solution)/shard_map/ppermute | solution.py:19
  206.0 26.0 %collective-permute-start.13 = (s16[16,72,512]{2,1,0:T(8,128)(2,1)}, s16[16,72,512]{2,1,0:T(8,128)(2,1)}, u32[]{:S(2)}, u32[]{:S(2)}) collective-permute-start(s16[16,72,512]{2,1,0:T(8,128)(2,1)} %slice_dynamic-update-slice_fusion), channel_id=1, source_target_pairs={{0,16},{16,0},{1,17},{17,1},{2,18},{18,2},{3,19},{19,3},{4,20},{20... | collective-permute-start | bytes 3538952 | tf_op jit(solution)/shard_map/ppermute | solution.py:23
  216.8 12.5 %copy-start.18 = (s32[1024]{0:T(1024)S(1)}, s32[1024]{0:T(1024)}, u32[]{:S(2)}) copy-start(s32[1024]{0:T(1024)} %param.9) | copy-start | bytes 12292
  217.9 30.6 %all-to-all-start.2 = ((s16[16,72,512]{2,1,0:T(8,128)(2,1)}), s16[16,72,512]{2,1,0:T(8,128)(2,1)S(1)}, u32[]{:S(2)}, u32[]{:S(2)}) async-start(s16[16,72,512]{2,1,0:T(8,128)(2,1)} %pad_add_fusion.1), calls=%async_computation.2 | async-start | bytes 2359296 | tf_op jit(solution)/shard_map/all_to_all | solution.py:122
  252.5 9.3 %copy-start.19 = (s16[2,16,1]{1,0,2:T(2,128)(2,1)S(1)}, s16[2,16,1]{1,0,2:T(2,128)(2,1)}, u32[]{:S(2)}) copy-start(s16[2,16,1]{1,0,2:T(2,128)(2,1)} %stack.224) | copy-start | bytes 196
  252.5 9.3 %copy-start.20 = (s16[2,16,1]{1,0,2:T(2,128)(2,1)S(1)}, s16[2,16,1]{1,0,2:T(2,128)(2,1)}, u32[]{:S(2)}) copy-start(s16[2,16,1]{1,0,2:T(2,128)(2,1)} %stack.223) | copy-start | bytes 196
  254.3 25.9 %all-to-all-start.3 = ((s16[32,72,256]{2,1,0:T(8,128)(2,1)}), s16[32,72,256]{2,1,0:T(8,128)(2,1)S(1)}, u32[]{:S(2)}, u32[]{:S(2)}) async-start(s16[32,72,256]{2,1,0:T(8,128)(2,1)} %bitcast.72), calls=%async_computation.3 | async-start | bytes 2359296 | tf_op jit(solution)/shard_map/all_to_all | solution.py:126
  263.6 2.3 copy-start.16
  263.6 2.3 copy-start.17
  291.7 2.9 copy-start.6
  (8 other events, 16.0 us)
